TPU v7x, 256 devices: a whole 4x4x8 slice. The times are simulated.
256 devices in a mesh: section: 8 (over y, core), seq: 32 (over x, z).
Axes of the slice: x: 4, y: 4, z: 8, core: 2. Of those that a mesh axis runs over, the one named last changes fastest.
Arguments:
- query: bfloat16 [8, 8192, 3072], P('section', 'seq'), may hold values from -60 to 60
- keys: bfloat16 [8, 8192, 1024], P('section', 'seq'), may hold values from -6 to 6
- values: bfloat16 [8, 8192, 1024], P('section', 'seq'), may hold values from -6 to 6
- documents: int32 [8, 64], P('section'), may hold values from 0 to 7, never falling along the last dimension, each value on 1 to 48 neighbouring positions
- retrieval_heads: int32 [8, 2], P('section'), may hold values from 0 to 7, as said below
Outputs:
- next_input: bfloat16 [8, 8192, 3072], P('section', 'seq')
Inputs may be any that keep to these rules, and one draw needn't show every extreme that they name: `documents`: document numbers never fall along a group; every document 0 to 7 occupies 1 to 48 consecutive blocks, and one occupies exactly 48. `retrieval_heads`: each section lists 2 different key and value heads.
All inputs are finite; a program needn't handle non-finite values.
Results may differ from a plain program's by a relative error of at most 0.0041.
Values may be sent and summed in bfloat16 or wider, within the bound.
A program may use at most 128 MiB of HBM per device.

v0:
```python
import math

import jax
import jax.numpy as jnp
from jax import lax
from jax.sharding import PartitionSpec as P

KVH = 8
HEAD_SIZE = 128
RKV = 2
BLK = 128
WBLOCKS = 8
RUNNING_KV_HEADS = 6
GQ = 3


def from_behind(shard, axis, by):
    length = lax.axis_size(axis)
    return lax.ppermute(shard, axis, [(i, (i + by) % length) for i in range(length)])


def broadcast(shard, axis, root):
    mine = lax.axis_index(axis) == root
    return lax.psum(jnp.where(mine, shard, jnp.zeros_like(shard)), axis)


def doc_of(positions, doc_row):
    count = doc_row.shape[0]
    hits = (positions // BLK)[:, None] == jnp.arange(count, dtype=jnp.int32)[None, :]
    return jnp.sum(jnp.where(hits, doc_row[None, :], 0), axis=1)


def shards(query, keys, values, documents, retrieval_heads):
    row_indices = query.shape[1]
    half_rows = row_indices // 2
    width_seq = lax.axis_size("seq")
    me = lax.axis_index("seq")
    local_rows = jnp.arange(row_indices, dtype=jnp.int32)
    qpos = (local_rows // half_rows * width_seq + me) * half_rows + local_rows % half_rows
    doc_row = documents[0]
    qdoc = doc_of(qpos, doc_row)
    qblock = qpos // BLK
    scale = 1.0 / math.sqrt(HEAD_SIZE)
    heads_row = retrieval_heads[0]
    picked = heads_row[:, None] == jnp.arange(KVH, dtype=jnp.int32)[None, :]
    chosen = jnp.any(picked, axis=0)
    remaining_parts = 1 - chosen.astype(jnp.int32)
    section_rank = jnp.cumsum(remaining_parts) - 1
    other_parts = (remaining_parts[None, :] == 1) & (
        section_rank[None, :] == jnp.arange(RUNNING_KV_HEADS, dtype=jnp.int32)[:, None]
    )
    pick_ret = picked.astype(jnp.bfloat16)
    pick_str = other_parts.astype(jnp.bfloat16)
    q_four = query[0].reshape(row_indices, KVH, GQ, HEAD_SIZE)
    k_three = keys[0].reshape(row_indices, KVH, HEAD_SIZE)
    v_three = values[0].reshape(row_indices, KVH, HEAD_SIZE)
    q_ret = jnp.einsum(
        "rgjd,hg->rhjd", q_four, pick_ret, preferred_element_type=jnp.float32
    ).astype(jnp.bfloat16)
    q_str = jnp.einsum(
        "rgjd,hg->rhjd", q_four, pick_str, preferred_element_type=jnp.float32
    ).astype(jnp.bfloat16)
    kv_ret = jnp.concatenate(
        [
            jnp.einsum(
                "rgd,hg->rhd", k_three, pick_ret, preferred_element_type=jnp.float32
            ).reshape(row_indices, RKV * HEAD_SIZE),
            jnp.einsum(
                "rgd,hg->rhd", v_three, pick_ret, preferred_element_type=jnp.float32
            ).reshape(row_indices, RKV * HEAD_SIZE),
        ],
        axis=1,
    ).astype(jnp.bfloat16)
    kv_str = jnp.concatenate(
        [
            jnp.einsum(
                "rgd,hg->rhd", k_three, pick_str, preferred_element_type=jnp.float32
            ).reshape(row_indices, RUNNING_KV_HEADS * HEAD_SIZE),
            jnp.einsum(
                "rgd,hg->rhd", v_three, pick_str, preferred_element_type=jnp.float32
            ).reshape(row_indices, RUNNING_KV_HEADS * HEAD_SIZE),
        ],
        axis=1,
    ).astype(jnp.bfloat16)
    init = (
        jnp.full((RKV, GQ, row_indices), -1e30, jnp.float32),
        jnp.zeros((RKV, GQ, row_indices), jnp.float32),
        jnp.zeros((RKV, GQ, row_indices, HEAD_SIZE), jnp.float32),
    )
    piece = lax.all_gather(kv_ret, "seq", axis=0, tiled=True)
    global_rows = jnp.arange(piece.shape[0], dtype=jnp.int32)
    inside = global_rows % row_indices
    key_positions = (
        inside // half_rows * width_seq + global_rows // row_indices
    ) * half_rows + inside % half_rows
    count = piece.shape[0]
    width = math.gcd(count, 512)

    def one_block(index_value, state):
        kstart = index_value * width
        block = lax.dynamic_slice_in_dim(piece, kstart, width, 0)
        kpos = lax.dynamic_slice_in_dim(key_positions, kstart, width, 0)
        kdoc = doc_of(kpos, doc_row)
        allow = (
            (kpos[None, :] >= 0)
            & (kpos[None, :] <= qpos[:, None])
            & (kdoc[None, :] == qdoc[:, None])
        )

        def attend(inner):
            best, total, accum = inner
            key_part = block[:, : RKV * HEAD_SIZE].reshape(width, RKV, HEAD_SIZE)
            value_slice = block[:, RKV * HEAD_SIZE :].reshape(width, RKV, HEAD_SIZE)
            score = (
                jnp.einsum("rhjd,khd->hjrk", q_ret, key_part, preferred_element_type=jnp.float32)
                * scale
            )
            score = jnp.where(allow, score, -1e30)
            fresh = jnp.maximum(best, jnp.max(score, axis=-1))
            weight = jnp.where(allow, jnp.exp(score - fresh[..., None]), 0.0)
            factor = jnp.exp(best - fresh)
            total = total * factor + jnp.sum(weight, axis=-1)
            accum = accum * factor[..., None] + jnp.einsum(
                "hjrk,khd->hjrd",
                weight.astype(jnp.bfloat16),
                value_slice,
                preferred_element_type=jnp.float32,
            )
            return (fresh, total, accum)

        return lax.cond(jnp.any(allow), attend, lambda inner: inner, state)

    state = lax.fori_loop(0, count // width, one_block, init)
    retrieved = (state[2] / state[1][..., None]).astype(jnp.bfloat16)
    reach_window = ((WBLOCKS - 1) * BLK + half_rows - 1) // half_rows
    half_index = jnp.arange(half_rows, dtype=jnp.int32)
    near_parts = []
    near_positions = []
    for distance in range(reach_window, 0, -1):
        arrived = from_behind(kv_str, "seq", distance)
        source = me - distance
        near_parts.append(arrived[:half_rows])
        near_positions.append(source * half_rows + half_index)
        near_parts.append(jnp.where(source >= 0, arrived[half_rows:], arrived[:half_rows]))
        near_positions.append((width_seq + source) * half_rows + half_index)
    near_parts.append(kv_str)
    near_positions.append(qpos)
    sink = broadcast(kv_str[:BLK], "seq", 0)
    near = jnp.concatenate(near_parts, axis=0)
    wpos = jnp.concatenate(near_positions, axis=0)
    allow_w = (
        (wpos[None, :] >= 0)
        & (wpos[None, :] <= qpos[:, None])
        & (qblock[:, None] - wpos[None, :] // BLK < WBLOCKS)
    )
    allow_s = jnp.broadcast_to((qblock >= WBLOCKS)[:, None], (row_indices, BLK))
    allow = jnp.concatenate([allow_s, allow_w], axis=1)
    lookup_table = jnp.concatenate([sink, near], axis=0)

    def window_head(index_value):
        key_part = lax.dynamic_slice_in_dim(lookup_table, index_value * HEAD_SIZE, HEAD_SIZE, 1)
        value_slice = lax.dynamic_slice_in_dim(
            lookup_table, (RUNNING_KV_HEADS + index_value) * HEAD_SIZE, HEAD_SIZE, 1
        )
        q_head = lax.dynamic_index_in_dim(q_str, index_value, 1, keepdims=False)
        score = (
            jnp.einsum("rjd,kd->jrk", q_head, key_part, preferred_element_type=jnp.float32) * scale
        )
        score = jnp.where(allow[None], score, -1e30)
        top = jnp.max(score, axis=-1, keepdims=True)
        weight = jnp.where(allow[None], jnp.exp(score - top), 0.0)
        total = jnp.sum(weight, axis=-1)
        mixed = jnp.einsum(
            "jrk,kd->jrd",
            weight.astype(jnp.bfloat16),
            value_slice,
            preferred_element_type=jnp.float32,
        )
        return (mixed / total[..., None]).astype(jnp.bfloat16)

    read_values = lax.map(window_head, jnp.arange(RUNNING_KV_HEADS, dtype=jnp.int32))
    combined = jnp.einsum("hjrd,hg->rgjd", retrieved, pick_ret, preferred_element_type=jnp.float32)
    combined = combined + jnp.einsum(
        "hjrd,hg->rgjd", read_values, pick_str, preferred_element_type=jnp.float32
    )
    combined = combined.astype(jnp.bfloat16).reshape(row_indices, KVH * GQ * HEAD_SIZE)
    moved = from_behind(combined, "section", 1)
    return moved[None]


def solution(mesh):
    placed = (
        P("section", "seq", None),
        P("section", "seq", None),
        P("section", "seq", None),
        P("section", None),
        P("section", None),
    )
    return jax.shard_map(
        shards, mesh=mesh, in_specs=placed, out_specs=P("section", "seq", None), check_vma=False
    )
```

profile of v0, /device:TPU:1, one launch (start us, length us, event | category | flops | bytes accessed | tf_op | source)
XLA Modules:
  0.0 557.6 jit_solution(12346209305176453655)
XLA Ops:
  14.0 6.4 %collective-permute-start = (bf16[256,1536]{0,1:T(8,128)(2,1)}, bf16[256,1536]{0,1:T(8,128)(2,1)}, u32[]{:S(2)}, u32[]{:S(2)}) collective-permute-start(bf16[256,1536]{0,1:T(8,128)(2,1)} %pad_maximum_fusion), channel_id=1, source_target_pairs={{0,7},{1,8},{2,9},{3,10},{4,11},{5,12},{6,13},{7,14},{8,15},{9,16}... | collective-permute-start | bytes 2359304 | tf_op jit(solution)/shard_map/ppermute | solution.py:19
  23.2 5.1 collective-permute-start.3
  36.1 238.2 %all-reduce.2.cloned.1.call-done = bf16[128,1536]{0,1:T(8,128)(2,1)} async-done(((bf16[128,1536]{0,1:T(8,128)(2,1)}), bf16[128,1536]{0,1:T(8,128)(2,1)}) %all-reduce.2.cloned.1.call-update) | async-done | bytes 393232 | tf_op jit(solution)/shard_map/psum | solution.py:24
  297.8 10.3 %collective-permute-done.5 = bf16[256,1536]{0,1:T(8,128)(2,1)S(1)} collective-permute-done((bf16[256,1536]{0,1:T(8,128)(2,1)}, bf16[256,1536]{0,1:T(8,128)(2,1)S(1)}, u32[]{:S(2)}, u32[]{:S(2)}) %collective-permute-start.5) | collective-permute-done | bytes 786464 | tf_op jit(solution)/shard_map/ppermute | solution.py:19
  309.8 30.4 %collective-permute-done.6 = bf16[256,1536]{0,1:T(8,128)(2,1)S(1)} collective-permute-done((bf16[256,1536]{0,1:T(8,128)(2,1)}, bf16[256,1536]{0,1:T(8,128)(2,1)S(1)}, u32[]{:S(2)}, u32[]{:S(2)}) %collective-permute-start.6) | collective-permute-done | bytes 786464 | tf_op jit(solution)/shard_map/ppermute | solution.py:19
  343.1 9.9 %copy.48 = bf16[2176,1536]{1,0:T(8,128)(2,1)} copy(bf16[2176,1536]{0,1:T(8,128)(2,1)} %constant_dynamic-update-slice_fusion.1) | data formatting | bytes 13369344 | tf_op jit(solution)/shard_map/while | solution.py:181
  353.0 82.2 %while.30 = (s32[]{:T(128)}, bf16[6,3,256,128]{3,2,1,0:T(8,128)(2,1)S(1)}, pred[256,2176]{0,1:T(8,128)(4,1)}, s32[6]{0:T(128)S(1)}, bf16[2176,1536]{1,0:T(8,128)...) while((s32[]{:T(128)}, ...), condition=%wide.region_15.16_spmd, body=%wide.region_12.15_spmd.sunk | while | flops 1300370432 | bytes 4497163 | solution.py:181
  356.1 4.6 fusion.188
  360.7 5.9 %fusion.189 = bf16[6,3,256,128]{3,2,1,0:T(8,128)(2,1)S(1)} fusion(bf16[6,3,256,128]{3,2,1,0:T(8,128)(2,1)S(1)} %get-tuple-element.629, s32[]{:T(128)} %get-tuple-element.628, pred[256,2176]{0,1:T(8,128)(4,1)} %get-tuple-element.641, bf16[2176,1536]{1,0:T(8,128)(2,1)} %get-tuple-element.643, s32[]{:T(128)S(6)} %select_n.409, s32[]{:T(128)S(6)} %select_n.410, ...), kind=kOutput, calls=%fused_computation.27.clone.1 | convolution fusion | flops 864193408 | bytes 2626060 | tf_op jit(solution)/shard_map/while/body/eval_jaxpr/jrk,kd->jrd/dot_general | solution.py:173
  369.9 4.6 fusion.188
  374.5 5.9 %fusion.189 = bf16[6,3,256,128]{3,2,1,0:T(8,128)(2,1)S(1)} fusion(bf16[6,3,256,128]{3,2,1,0:T(8,128)(2,1)S(1)} %get-tuple-element.629, s32[]{:T(128)} %get-tuple-element.628, pred[256,2176]{0,1:T(8,128)(4,1)} %get-tuple-element.641, bf16[2176,1536]{1,0:T(8,128)(2,1)} %get-tuple-element.643, s32[]{:T(128)S(6)} %select_n.409, s32[]{:T(128)S(6)} %select_n.410, ...), kind=kOutput, calls=%fused_computation.27.clone.1 | convolution fusion | flops 864193408 | bytes 2626060 | tf_op jit(solution)/shard_map/while/body/eval_jaxpr/jrk,kd->jrd/dot_general | solution.py:173
  383.6 4.6 fusion.188
  388.2 5.9 %fusion.189 = bf16[6,3,256,128]{3,2,1,0:T(8,128)(2,1)S(1)} fusion(bf16[6,3,256,128]{3,2,1,0:T(8,128)(2,1)S(1)} %get-tuple-element.629, s32[]{:T(128)} %get-tuple-element.628, pred[256,2176]{0,1:T(8,128)(4,1)} %get-tuple-element.641, bf16[2176,1536]{1,0:T(8,128)(2,1)} %get-tuple-element.643, s32[]{:T(128)S(6)} %select_n.409, s32[]{:T(128)S(6)} %select_n.410, ...), kind=kOutput, calls=%fused_computation.27.clone.1 | convolution fusion | flops 864193408 | bytes 2626060 | tf_op jit(solution)/shard_map/while/body/eval_jaxpr/jrk,kd->jrd/dot_general | solution.py:173
  397.3 4.6 fusion.188
  401.9 5.9 %fusion.189 = bf16[6,3,256,128]{3,2,1,0:T(8,128)(2,1)S(1)} fusion(bf16[6,3,256,128]{3,2,1,0:T(8,128)(2,1)S(1)} %get-tuple-element.629, s32[]{:T(128)} %get-tuple-element.628, pred[256,2176]{0,1:T(8,128)(4,1)} %get-tuple-element.641, bf16[2176,1536]{1,0:T(8,128)(2,1)} %get-tuple-element.643, s32[]{:T(128)S(6)} %select_n.409, s32[]{:T(128)S(6)} %select_n.410, ...), kind=kOutput, calls=%fused_computation.27.clone.1 | convolution fusion | flops 864193408 | bytes 2626060 | tf_op jit(solution)/shard_map/while/body/eval_jaxpr/jrk,kd->jrd/dot_general | solution.py:173
  411.0 4.6 fusion.188
  415.6 5.9 %fusion.189 = bf16[6,3,256,128]{3,2,1,0:T(8,128)(2,1)S(1)} fusion(bf16[6,3,256,128]{3,2,1,0:T(8,128)(2,1)S(1)} %get-tuple-element.629, s32[]{:T(128)} %get-tuple-element.628, pred[256,2176]{0,1:T(8,128)(4,1)} %get-tuple-element.641, bf16[2176,1536]{1,0:T(8,128)(2,1)} %get-tuple-element.643, s32[]{:T(128)S(6)} %select_n.409, s32[]{:T(128)S(6)} %select_n.410, ...), kind=kOutput, calls=%fused_computation.27.clone.1 | convolution fusion | flops 864193408 | bytes 2626060 | tf_op jit(solution)/shard_map/while/body/eval_jaxpr/jrk,kd->jrd/dot_general | solution.py:173
  424.7 4.6 fusion.188
  429.2 5.9 %fusion.189 = bf16[6,3,256,128]{3,2,1,0:T(8,128)(2,1)S(1)} fusion(bf16[6,3,256,128]{3,2,1,0:T(8,128)(2,1)S(1)} %get-tuple-element.629, s32[]{:T(128)} %get-tuple-element.628, pred[256,2176]{0,1:T(8,128)(4,1)} %get-tuple-element.641, bf16[2176,1536]{1,0:T(8,128)(2,1)} %get-tuple-element.643, s32[]{:T(128)S(6)} %select_n.409, s32[]{:T(128)S(6)} %select_n.410, ...), kind=kOutput, calls=%fused_computation.27.clone.1 | convolution fusion | flops 864193408 | bytes 2626060 | tf_op jit(solution)/shard_map/while/body/eval_jaxpr/jrk,kd->jrd/dot_general | solution.py:173
  435.3 92.2 %while.31 = (s32[]{:T(128)}, f32[2,3,256]{2,1,0:T(4,128)S(1)}, f32[2,3,256]{2,1,0:T(4,128)S(1)}, f32[2,3,256,128]{3,2,1,0:T(8,128)S(1)}, s32[8192]{0:T(1024)S(1)...) while((s32[]{:T(128)}, f32[2,3,256]{2,1,0:T(4,128)S(1)}, ...), condition=%wide.region_8.9_spmd.clone, body=%wide.region_1.8_spmd.clone.sunk | while | flops 414038528 | bytes 13619781 | solution.py:133
  437.0 4.0 conditional.3
  442.7 4.0 conditional.3
  454.2 4.0 conditional.3
  531.4 17.7 %collective-permute-done.7 = bf16[256,3072]{0,1:T(8,128)(2,1)S(1)} collective-permute-done((bf16[256,3072]{0,1:T(8,128)(2,1)}, bf16[256,3072]{0,1:T(8,128)(2,1)S(1)}, u32[]{:S(2)}, u32[]{:S(2)}) %collective-permute-start.7) | collective-permute-done | bytes 1572896 | tf_op jit(solution)/shard_map/ppermute | solution.py:19
  (320 shorter events, 188.7 us)
Async XLA Ops:
  6.5 2.9 copy-start.5
  6.5 267.7 %all-reduce.2.cloned.1.call-start = ((), (), s32[]{:S(2)}) async-start(), calls=%async_computation.1 | async-start | bytes 786432 | tf_op jit(solution)/shard_map/psum | solution.py:24
  8.7 2.6 copy-start.7
  9.4 3.6 copy-start
  10.3 19.8 %copy-start.2 = (bf16[256,6,128]{0,2,1:T(8,128)(2,1)}, bf16[256,6,128]{0,2,1:T(8,128)(2,1)S(1)}, u32[]{:S(2)}) copy-start(bf16[256,6,128]{0,2,1:T(8,128)(2,1)S(1)} %copy.45) | copy-start | bytes 1179652
  11.2 424.0 %all-gather.2.cloned.1.call-start = ((), (), s32[]{:S(2)}) async-start(), calls=%async_computation | async-start | bytes 8650752 | tf_op jit(solution)/shard_map/all_gather | solution.py:90
  14.0 262.1 %collective-permute-start = (bf16[256,1536]{0,1:T(8,128)(2,1)}, bf16[256,1536]{0,1:T(8,128)(2,1)}, u32[]{:S(2)}, u32[]{:S(2)}) collective-permute-start(bf16[256,1536]{0,1:T(8,128)(2,1)} %pad_maximum_fusion), channel_id=1, source_target_pairs={{0,7},{1,8},{2,9},{3,10},{4,11},{5,12},{6,13},{7,14},{8,15},{9,16}... | collective-permute-start | bytes 2359304 | tf_op jit(solution)/shard_map/ppermute | solution.py:19
  20.4 260.9 %collective-permute-start.1 = (bf16[256,1536]{0,1:T(8,128)(2,1)}, bf16[256,1536]{0,1:T(8,128)(2,1)}, u32[]{:S(2)}, u32[]{:S(2)}) collective-permute-start(bf16[256,1536]{0,1:T(8,128)(2,1)} %pad_maximum_fusion), channel_id=1, source_target_pairs={{0,6},{1,7},{2,8},{3,9},{4,10},{5,11},{6,12},{7,13},{8,14},{9,15},... | collective-permute-start | bytes 2359304 | tf_op jit(solution)/shard_map/ppermute | solution.py:19
  22.5 263.6 %collective-permute-start.2 = (bf16[256,1536]{0,1:T(8,128)(2,1)}, bf16[256,1536]{0,1:T(8,128)(2,1)}, u32[]{:S(2)}, u32[]{:S(2)}) collective-permute-start(bf16[256,1536]{0,1:T(8,128)(2,1)} %pad_maximum_fusion), channel_id=1, source_target_pairs={{0,5},{1,6},{2,7},{3,8},{4,9},{5,10},{6,11},{7,12},{8,13},{9,14},{... | collective-permute-start | bytes 2359304 | tf_op jit(solution)/shard_map/ppermute | solution.py:19
  23.2 266.8 %collective-permute-start.3 = (bf16[256,1536]{0,1:T(8,128)(2,1)}, bf16[256,1536]{0,1:T(8,128)(2,1)}, u32[]{:S(2)}, u32[]{:S(2)}) collective-permute-start(bf16[256,1536]{0,1:T(8,128)(2,1)} %pad_maximum_fusion), channel_id=1, source_target_pairs={{0,4},{1,5},{2,6},{3,7},{4,8},{5,9},{6,10},{7,11},{8,12},{9,13},{1... | collective-permute-start | bytes 2359304 | tf_op jit(solution)/shard_map/ppermute | solution.py:19
  28.3 265.5 %collective-permute-start.4 = (bf16[256,1536]{0,1:T(8,128)(2,1)}, bf16[256,1536]{0,1:T(8,128)(2,1)}, u32[]{:S(2)}, u32[]{:S(2)}) collective-permute-start(bf16[256,1536]{0,1:T(8,128)(2,1)} %pad_maximum_fusion), channel_id=1, source_target_pairs={{0,3},{1,4},{2,5},{3,6},{4,7},{5,8},{6,9},{7,10},{8,11},{9,12},{10... | collective-permute-start | bytes 2359304 | tf_op jit(solution)/shard_map/ppermute | solution.py:19
  31.2 1.0 copy-start.8
  31.9 3.0 copy-start.6
  276.0 32.0 %collective-permute-start.5 = (bf16[256,1536]{0,1:T(8,128)(2,1)}, bf16[256,1536]{0,1:T(8,128)(2,1)S(1)}, u32[]{:S(2)}, u32[]{:S(2)}) collective-permute-start(bf16[256,1536]{0,1:T(8,128)(2,1)} %pad_maximum_fusion), channel_id=1, source_target_pairs={{0,2},{1,3},{2,4},{3,5},{4,6},{5,7},{6,8},{7,9},{8,10},{9,11},{10,... | collective-permute-start | bytes 2359304 | tf_op jit(solution)/shard_map/ppermute | solution.py:19
  281.3 58.9 %collective-permute-start.6 = (bf16[256,1536]{0,1:T(8,128)(2,1)}, bf16[256,1536]{0,1:T(8,128)(2,1)S(1)}, u32[]{:S(2)}, u32[]{:S(2)}) collective-permute-start(bf16[256,1536]{0,1:T(8,128)(2,1)} %pad_maximum_fusion), channel_id=1, source_target_pairs={{0,1},{1,2},{2,3},{3,4},{4,5},{5,6},{6,7},{7,8},{8,9},{9,10},{10,1... | collective-permute-start | bytes 2359304 | tf_op jit(solution)/shard_map/ppermute | solution.py:19
  293.9 48.2 %copy-start.1 = (bf16[256,6,128]{0,2,1:T(8,128)(2,1)S(1)}, bf16[256,6,128]{0,2,1:T(8,128)(2,1)}, u32[]{:S(2)}) copy-start(bf16[256,6,128]{0,2,1:T(8,128)(2,1)} %copy-done) | copy-start | bytes 1179652
  293.9 48.2 %copy-start.3 = (bf16[256,6,128]{0,2,1:T(8,128)(2,1)S(1)}, bf16[256,6,128]{0,2,1:T(8,128)(2,1)}, u32[]{:S(2)}) copy-start(bf16[256,6,128]{0,2,1:T(8,128)(2,1)} %copy-done.2) | copy-start | bytes 1179652
  343.1 9.9 %copy-start.4 = (bf16[6,3,256,128]{3,2,1,0:T(8,128)(2,1)S(1)}, bf16[6,3,256,128]{3,2,1,0:T(8,128)(2,1)}, u32[]{:S(2)}) copy-start(bf16[6,3,256,128]{3,2,1,0:T(8,128)(2,1)} %custom-call.2) | copy-start | bytes 3538948
  531.4 17.7 %collective-permute-start.7 = (bf16[256,3072]{0,1:T(8,128)(2,1)}, bf16[256,3072]{0,1:T(8,128)(2,1)S(1)}, u32[]{:S(2)}, u32[]{:S(2)}) collective-permute-start(bf16[256,3072]{0,1:T(8,128)(2,1)} %bitcast.169), channel_id=1, source_target_pairs={{0,32},{32,64},{64,96},{96,128},{128,160},{160,192},{192,224},{224... | collective-permute-start | bytes 4718600 | tf_op jit(solution)/shard_map/ppermute | solution.py:19
Sparse Core Ops, SparseCore 0:
  11.3 262.8 all-reduce.1
  277.0 123.5 all-gather.1
where the time goes:
time: 562 us; the launch traced here: 558 us
  waiting for transfers between devices  297 us (53%)
  matrix products  101 us (18%)
  local copies, waits for them, and re-layouts  52.2 us (9%)
  other arithmetic  50.4 us (9%)
  loops' own time  26.5 us (5%)
  starting transfers between devices  16.7 us (3%)
  between operations  13.9 us (2%)
    psum x1, waiting for transfers between devices, broadcast(): return lax.psum(jnp.where(mine, shard, jnp.zeros_like(shard)), axis)  238 us
    ppermute x8, waiting for transfers between devices, from_behind(): lax.ppermute(shard, axis, [(i, (i + by) % length) for i in range(length)])  58.4 us
    dot_general x6, matrix products, window_head(): jnp.einsum('jrk,kd->jrd', weight.astype(jnp.bfloat16), value_slice, prefe...  35.4 us
    sub x6, matrix products, window_head(): weight = jnp.where(allow[None], jnp.exp(score - top), 0.0)  27.5 us
    dot_general x16, matrix products, attend(): jnp.einsum('hjrk,khd->hjrd', weight.astype(jnp.bfloat16), value_slice, pr...  22.1 us
    slice x16, local copies, waits for them, and re-layouts, attend(): value_slice = block[:, RKV * HEAD_SIZE:].reshape(width, RKV, HEAD_SIZE)  17.2 us
    ppermute x8, starting transfers between devices, from_behind(): lax.ppermute(shard, axis, [(i, (i + by) % length) for i in range(length)])  16.7 us
    unnamed x30, local copies, waits for them, and re-layouts  15.7 us
  transfers between devices with their start and end apart: 10, of which 4 were waited for; matrix products, arithmetic and copies ran while one was open for 20% of the time, Pallas kernels for 0%

commit v1 on v0

v1 whole, which is shorter than its diff:
```python
import math

import jax
import jax.numpy as jnp
from jax import lax
from jax.experimental import pallas as pl
from jax.experimental.pallas import tpu as pltpu
from jax.sharding import PartitionSpec as P

KVH = 8
HEAD_SIZE = 128
RKV = 2
BLK = 128
WBLOCKS = 8
RUN = KVH - RKV
GQ = 3
ROWS = GQ * BLK
NZ = 8
NX = 4
LEAD = 2
NEG = -1e30
LOW = -1e29
CEXP = math.log2(math.e) / math.sqrt(HEAD_SIZE)
MESH = pl.DeviceIdType.MESH


def dot_nt(a, b):
    return lax.dot_general(a, b, (((1,), (1,)), ((), ())), preferred_element_type=jnp.float32)


def kernel(
    docs, heads, q_ref, k_ref, v_ref, out_ref,
    kv, sink, qx, po, pr, st, sr, res, outst, s_ref,
    ksend, krecv, ssend, srecv, qsend, qrecv, psend, precv, tsend, trecv, osend, orecv,
):
    sec = lax.axis_index("section")
    me = lax.axis_index("seq")
    nsec = lax.axis_size("section")
    nseq = NX * NZ
    x, z = me // NZ, me % NZ
    lo = jnp.minimum(heads[0, 0], heads[0, 1])
    hi = jnp.maximum(heads[0, 0], heads[0, 1])

    row_next, row_prev = x * NZ + (z + 1) % NZ, x * NZ + (z + NZ - 1) % NZ
    pos_next, pos_prev = (me + 1) % nseq, (me + nseq - 1) % nseq
    pos_far, pos_back = (me + NZ - 1) % nseq, (me + nseq - NZ + 1) % nseq
    wrap_next = (me + 1) // nseq
    wrap_prev = 1 - (me + nseq - 1) // nseq
    wrap_far = (me + NZ - 1) // nseq

    def peer(c, kind):
        ret = c < RKV
        if kind == "next":
            return jnp.where(ret, row_next, pos_next), jnp.where(ret, 0, wrap_next)
        if kind == "prev":
            return jnp.where(ret, row_prev, pos_prev), jnp.where(ret, 0, wrap_prev)
        return jnp.where(ret, row_prev, pos_far), jnp.where(ret, 0, wrap_far)

    def block_copy(c, half, src, dh, dst, to):
        return pltpu.make_async_remote_copy(
            src_ref=kv.at[c, half, :, src], dst_ref=kv.at[c, dh, :, dst],
            send_sem=ksend.at[c, dst, half], recv_sem=krecv.at[c, dst, dh],
            device_id={"seq": to}, device_id_type=MESH,
        )

    def push(c, src, dst, kind):
        to, swap = peer(c, kind)
        for half in range(2):
            dh = swap if half == 0 else 1 - swap
            block_copy(c, half, src, dh, dst, to).start()

    def landed(c, slot):
        for half in range(2):
            block_copy(c, half, slot, half, slot, pos_next).wait_recv()
        if slot:
            give_sink(c, slot)

    def sink_copy(c, slot, r):
        return pltpu.make_async_remote_copy(
            src_ref=kv.at[c, 0, :, slot], dst_ref=sink.at[c - RKV],
            send_sem=ssend.at[c - RKV, r - 1], recv_sem=srecv.at[c - RKV],
            device_id={"seq": r * NZ + z}, device_id_type=MESH,
        )

    def give_sink(c, slot):
        @pl.when((x == 0) & (z == slot) & (c >= RKV))
        def _():
            for r in range(1, NX):
                sink_copy(c, slot, r).start()

    def q_copy(e):
        return pltpu.make_async_remote_copy(
            src_ref=qx.at[0], dst_ref=qx.at[e], send_sem=qsend.at[e - 1], recv_sem=qrecv.at[e - 1],
            device_id={"seq": (x + e) % NX * NZ + z}, device_id_type=MESH,
        )

    def part_copies(e, h):
        to = (x + NX - e) % NX * NZ + z
        return (
            pltpu.make_async_remote_copy(
                src_ref=po.at[e, h], dst_ref=pr.at[e - 1, h],
                send_sem=psend.at[e - 1, h], recv_sem=precv.at[e - 1, h],
                device_id={"seq": to}, device_id_type=MESH,
            ),
            pltpu.make_async_remote_copy(
                src_ref=st.at[e, h], dst_ref=sr.at[e - 1, h],
                send_sem=tsend.at[e - 1, h], recv_sem=trecv.at[e - 1, h],
                device_id={"seq": to}, device_id_type=MESH,
            ),
        )

    def out_copy(k):
        return pltpu.make_async_remote_copy(
            src_ref=outst.at[k], dst_ref=out_ref.at[:, pl.ds(pl.multiple_of(k * ROWS, 128), ROWS)],
            send_sem=osend.at[k], recv_sem=orecv.at[k],
            device_id={"section": (sec + 1) % nsec}, device_id_type=MESH,
        )

    def head_of(c):
        k = c - RKV
        g = k + (k >= lo).astype(jnp.int32)
        g = g + (g >= hi).astype(jnp.int32)
        return jnp.where(c == 0, heads[0, 0], jnp.where(c == 1, heads[0, 1], g))

    def place_of(g):
        run = RKV + g - (g > lo).astype(jnp.int32) - (g > hi).astype(jnp.int32)
        return jnp.where(g == heads[0, 0], 0, jnp.where(g == heads[0, 1], 1, run))

    barrier = pltpu.get_barrier_semaphore()
    near = [row_next, row_prev, pos_next, pos_prev, pos_far, pos_back]
    near += [(x + e) % NX * NZ + z for e in range(1, NX)]
    for to in near:
        pl.semaphore_signal(barrier, inc=1, device_id={"seq": to}, device_id_type=MESH)
    for by in (1, nsec - 1):
        pl.semaphore_signal(
            barrier, inc=1, device_id={"section": (sec + by) % nsec}, device_id_type=MESH
        )

    def columns(ref, half, g, width):
        rows = pl.ds(pl.multiple_of(half * BLK, BLK), BLK)
        return ref[rows, pl.ds(pl.multiple_of(g * width, HEAD_SIZE), width)]

    def own(ref, half, c, width):
        g = head_of(c)
        if isinstance(c, int) and c < RKV:
            out = columns(ref, half, 0, width)
            for other in range(1, KVH):
                out = lax.select(g == other, columns(ref, half, other, width), out)
            return out
        out = columns(ref, half, c - RKV, width)
        for other in (c - 1, c):
            out = lax.select(g == other, columns(ref, half, other, width), out)
        return out

    def stage(c, _):
        for half in range(2):
            kv[c, half, 0, 0] = own(k_ref, half, c, HEAD_SIZE)
            kv[c, half, 1, 0] = own(v_ref, half, c, HEAD_SIZE)
        return 0

    def stage_q(h):
        for half in range(2):
            rows = own(q_ref, half, h, ROWS)
            for j in range(GQ):
                qx[0, h, half, j * BLK : (j + 1) * BLK] = rows[:, j * HEAD_SIZE : (j + 1) * HEAD_SIZE]

    for c in range(RKV):
        stage(c, 0)
        stage_q(c)
    lax.fori_loop(RKV, KVH, stage, 0)

    pl.semaphore_wait(barrier, len(near) + 2)

    def first_sends(c):
        push(c, 0, 1, "next")
        push(c, 0, NZ - 1, "far")
        give_sink(c, 0)

    for c in range(LEAD):
        first_sends(c)
    for e in range(1, NX):
        q_copy(e).start()

    tri = lax.rem(lax.broadcasted_iota(jnp.int32, (ROWS, BLK), 0), BLK) >= lax.broadcasted_iota(
        jnp.int32, (ROWS, BLK), 1
    )

    def bias_of(ok):
        return jnp.where(ok, 0.0, NEG).astype(jnp.float32)

    def attend(queries, tiles):
        top, at, places = None, 0, []
        for keys, _, biases in tiles:
            s = dot_nt(queries, keys())
            for i, b in enumerate(biases):
                piece = s[:, i * BLK : (i + 1) * BLK] + b
                s_ref[:, at + i * BLK : at + (i + 1) * BLK] = piece
                top = piece if top is None else jnp.maximum(top, piece)
            places.append((at, len(biases) * BLK))
            at += len(biases) * BLK
        top = jnp.maximum(jnp.max(top, axis=1, keepdims=True), LOW)
        cut = top * CEXP
        total, mixed = None, None
        for (_, values, _), (at, width) in zip(tiles, places):
            w = jnp.exp2(s_ref[:, at : at + width] * CEXP - cut)
            for i in range(width // BLK):
                piece = w[:, i * BLK : (i + 1) * BLK]
                total = piece if total is None else total + piece
            part = jnp.dot(w.astype(jnp.bfloat16), values(), preferred_element_type=jnp.float32)
            mixed = part if mixed is None else mixed + part
        return top, jnp.sum(total, axis=1, keepdims=True), mixed

    def pair(c, half, which, i):
        return lambda: kv[c, half, which, 2 * i : 2 * i + 2].reshape(2 * BLK, HEAD_SIZE)

    def running(c, half):
        k = c - RKV
        up = half == 1
        rows = own(q_ref, half, c, ROWS)
        queries = jnp.concatenate(
            [rows[:, j * HEAD_SIZE : (j + 1) * HEAD_SIZE] for j in range(GQ)], axis=0
        )
        tiles = [(lambda: sink[k, 0], lambda: sink[k, 1], [bias_of(up | (me >= WBLOCKS))])]
        for i in range(NZ // 2):
            biases = [bias_of(up | (me >= d)) for d in (2 * i, 2 * i + 1)]
            if i == 0:
                biases[0] = jnp.where(tri, 0.0, NEG)
            tiles.append((pair(c, half, 0, i), pair(c, half, 1, i), biases))
        _, total, mixed = attend(queries, tiles)
        out = (mixed / total).astype(jnp.bfloat16)
        for j in range(GQ):
            res[c, pl.ds(pl.multiple_of(half * BLK, BLK), BLK), j * HEAD_SIZE : (j + 1) * HEAD_SIZE] = out[
                j * BLK : (j + 1) * BLK
            ]

    def retrieval(h, e):
        qrow = (x + NX - e) % NX
        for half in range(2):
            i_blk = half * nseq + qrow * NZ + z
            i_doc = docs[0, i_blk]
            tiles = []
            for khalf in range(half + 1):
                for i in range(NZ // 2):
                    biases = []
                    for d in (2 * i, 2 * i + 1):
                        j_blk = khalf * nseq + x * NZ + (z + NZ - d) % NZ
                        b = bias_of((docs[0, j_blk] == i_doc) & (j_blk <= i_blk))
                        if d == 0 and khalf == half:
                            b = jnp.where(tri | (j_blk < i_blk), b, NEG)
                        biases.append(b)
                    tiles.append((pair(h, khalf, 0, i), pair(h, khalf, 1, i), biases))
            top, total, mixed = attend(qx[e, h, half], tiles)
            po[e, h, half] = (mixed / jnp.where(total > 0.0, total, 1.0)).astype(jnp.bfloat16)
            for n, column in enumerate((top, total)):
                wide = jnp.broadcast_to(column, (ROWS, BLK))
                for j in range(GQ):
                    row = (half * GQ + j) * 2 + n
                    st[e, h, row : row + 1, :] = wide[j * BLK : (j + 1) * BLK].T[0:1]

        @pl.when(e > 0)
        def _():
            for copy in part_copies(e, h):
                copy.start()

    def combine(h):
        for e in range(1, NX):
            for copy in part_copies(e, h):
                copy.wait_recv()
        for half in range(2):
            for j in range(GQ):
                row = (half * GQ + j) * 2
                tops = [st[0, h, row : row + 1]] + [sr[e, h, row : row + 1] for e in range(NX - 1)]
                sums = [st[0, h, row + 1 : row + 2]] + [sr[e, h, row + 1 : row + 2] for e in range(NX - 1)]
                best = jnp.maximum(jnp.maximum(tops[0], tops[1]), jnp.maximum(tops[2], tops[3]))
                shares = [jnp.exp2((m - best) * CEXP) * l for m, l in zip(tops, sums)]
                whole = shares[0] + shares[1] + shares[2] + shares[3]
                at = slice(j * BLK, (j + 1) * BLK)
                parts = [po[0, h, half, at]] + [pr[e, h, half, at] for e in range(NX - 1)]
                out = None
                for share, part in zip(shares, parts):
                    weight = jnp.broadcast_to(share / whole, (BLK, BLK)).T
                    term = weight * part.astype(jnp.float32)
                    out = term if out is None else out + term
                res[h, half * BLK : (half + 1) * BLK, at] = out.astype(jnp.bfloat16)

    def give_out(k, _):
        place = place_of(k)
        out = res[0]
        for c in (1, jnp.clip(k, RKV, KVH - 1), jnp.clip(k + 1, RKV, KVH - 1), jnp.minimum(k + RKV, KVH - 1)):
            out = lax.select(place == c, res[c], out)
        outst[k] = out
        out_copy(k).start()
        return 0

    def micro(w, _):
        t, u = w // 2, w % 2

        def with_head(c, f):
            @pl.when((c >= 0) & (c < KVH))
            def _():
                f(c)

        @pl.when(u == 0)
        def _():
            with_head(t - 4, lambda c: landed(c, 4))

            def third(c):
                landed(c, 3)

                @pl.when(c < RKV)
                def _():
                    push(c, 3, 4, "next")

                landed(c, 5)

                @pl.when(c >= RKV)
                def _():
                    push(c, 5, 4, "prev")

            with_head(t - 3, third)

        @pl.when(u == 1)
        def _():
            def second(c):
                landed(c, 2)
                push(c, 2, 3, "next")
                landed(c, 6)
                push(c, 6, 5, "prev")

            with_head(t - 2, second)

            def first(c):
                landed(c, 1)
                push(c, 1, 2, "next")
                landed(c, 7)
                push(c, 7, 6, "prev")

            with_head(t - 1, first)
            with_head(t + LEAD, first_sends)

        @pl.when(w == 8)
        def _():
            for e in range(1, NX):
                q_copy(e).wait_recv()

        @pl.when((t >= 4) & (t < 8))
        def _():
            h = (t - 4) // 2
            e = (1 + (w - 8) % 4) % 4
            retrieval(h, e)

        half = 1 - u
        c = t - 4 - half

        @pl.when((c >= RKV) & (c < KVH))
        def _():
            @pl.when(half == 0)
            def _():
                @pl.when(x == 0)
                def _():
                    sink[c - RKV] = kv[c, 0, :, z]

                @pl.when(x > 0)
                def _():
                    sink_copy(c, 0, 1).wait_recv()

            running(c, half)

        @pl.when(w == 17)
        def _():
            lax.fori_loop(0, RKV, lambda h, _: (combine(h), 0)[1], 0)

        @pl.when((u == 0) & (t >= 9))
        def _():
            first = jnp.where(t == 9, 0, t - 7)
            last = jnp.where(t == 12, KVH, t - 6)
            lax.fori_loop(first, last, give_out, 0)

        return 0

    lax.fori_loop(0, 25, micro, 0)

    for k in range(KVH):
        out_copy(k).wait_recv()
        out_copy(k).wait_send()

    def finish(c, _):
        for slot in range(1, NZ):
            for half in range(2):
                block_copy(c, half, slot, half, slot, pos_next).wait_send()
        return 0

    lax.fori_loop(0, KVH, finish, 0)
    for e in range(1, NX):
        q_copy(e).wait_send()
        for h in range(RKV):
            for copy in part_copies(e, h):
                copy.wait_send()

    @pl.when(x == 0)
    def _():
        for c in range(RKV, KVH):
            for r in range(1, NX):
                sink_copy(c, 0, r).wait_send()


def shards(query, keys, values, documents, retrieval_heads):
    rows, width = query.shape[1:]
    bf, f32 = jnp.bfloat16, jnp.float32
    dma = pltpu.SemaphoreType.DMA
    vmem = pl.BlockSpec(memory_space=pltpu.VMEM)
    smem = pl.BlockSpec(memory_space=pltpu.SMEM)
    out = pl.pallas_call(
        kernel,
        out_shape=jax.ShapeDtypeStruct((rows, width), bf),
        in_specs=[smem, smem, vmem, vmem, vmem],
        out_specs=vmem,
        scratch_shapes=[
            pltpu.VMEM((KVH, 2, 2, NZ, BLK, HEAD_SIZE), bf),
            pltpu.VMEM((RUN, 2, BLK, HEAD_SIZE), bf),
            pltpu.VMEM((NX, RKV, 2, ROWS, HEAD_SIZE), bf),
            pltpu.VMEM((NX, RKV, 2, ROWS, HEAD_SIZE), bf),
            pltpu.VMEM((NX - 1, RKV, 2, ROWS, HEAD_SIZE), bf),
            pltpu.VMEM((NX, RKV, 16, BLK), f32),
            pltpu.VMEM((NX - 1, RKV, 16, BLK), f32),
            pltpu.VMEM((KVH, rows, ROWS), bf),
            pltpu.VMEM((KVH, rows, ROWS), bf),
            pltpu.VMEM((ROWS, 2 * NZ * BLK), f32),
            dma((KVH, NZ, 2)),
            dma((KVH, NZ, 2)),
            dma((RUN, NX - 1)),
            dma((RUN,)),
            dma((NX - 1,)),
            dma((NX - 1,)),
            dma((NX - 1, RKV)),
            dma((NX - 1, RKV)),
            dma((NX - 1, RKV)),
            dma((NX - 1, RKV)),
            dma((KVH,)),
            dma((KVH,)),
        ],
        compiler_params=pltpu.CompilerParams(
            collective_id=0, has_side_effects=True, vmem_limit_bytes=50 * 1024 * 1024
        ),
    )(documents, retrieval_heads, query[0], keys[0], values[0])
    return out[None]


def solution(mesh):
    placed = (
        P("section", "seq", None),
        P("section", "seq", None),
        P("section", "seq", None),
        P("section", None),
        P("section", None),
    )
    return jax.shard_map(
        shards, mesh=mesh, in_specs=placed, out_specs=P("section", "seq", None), check_vma=False
    )
```

time: 562 us -> 164 us (0.29)
  the two profiles are of different devices: /device:TPU:1 before, /device:TPU:10 now
where the time goes in v1:
time: 164 us
  Pallas kernels  159 us (97%)
  local copies, waits for them, and re-layouts  4.54 us (3%)
    pallas_call x1, Pallas kernels, shards(): pl.pallas_call(kernel, out_shape=jax.ShapeDtypeStruct((rows, width), bf),...  159 us
    unnamed x9, local copies, waits for them, and re-layouts  4.54 us

profile of v1, /device:TPU:10, one launch (start us, length us, event | category | flops | bytes accessed | tf_op | source)
XLA Modules:
  0.0 163.5 jit_solution(7957646297613961414)
XLA Ops:
  0.0 0.0 copy-start
  0.0 1.0 copy-done
  1.0 0.0 copy-start.1
  1.0 1.0 copy-done.1
  2.1 0.0 copy-start.2
  2.1 0.7 copy-done.2
  2.7 0.0 copy-start.3
  2.7 0.7 copy-done.3
  3.4 159.0 %shard_map.55 = bf16[256,3072]{1,0:T(8,128)(2,1)S(1)} custom-call(s32[1,64]{1,0:T(1,128)S(1)} %copy-done.2, s32[1,2]{1,0:T(1,128)S(1)} %copy-done.3, bf16[256,3072]{1,0:T(8,128)(2,1)} %bitcast.7, bf16[256,1024]{1,0:T(8,128)(2,1)S(1)} %bitcast.5, bf16[256,1024]{1,0:T(8,128)(2,1)S(1)} %bitcast.6), custom_call_target="tpu_custom_call" | custom-call | tf_op jit(solution)/shard_map/pallas_call | solution.py:413
  162.4 1.1 copy.7
Async XLA Ops:
  0.0 1.0 copy-start
  1.0 1.0 copy-start.1
  2.1 0.7 copy-start.2
  2.7 0.7 copy-start.3

commit v2 on v1

v2 whole, which is shorter than its diff:
```python
import math

import jax
import jax.numpy as jnp
from jax import lax
from jax.experimental import pallas as pl
from jax.experimental.pallas import tpu as pltpu
from jax.sharding import PartitionSpec as P

KVH = 8
HEAD_SIZE = 128
RKV = 2
BLK = 128
WBLOCKS = 8
RUN = KVH - RKV
GQ = 3
ROWS = GQ * BLK
NZ = 8
NX = 4
LEAD = 4
PLUS = 3
WAVES = 2 * KVH
LAG = 2
DONE = 1 + 3 * LAG
NEG = -1e30
LOW = -1e29
CEXP = math.log2(math.e) / math.sqrt(HEAD_SIZE)
MESH = pl.DeviceIdType.MESH


def dot_nt(a, b):
    return lax.dot_general(a, b, (((1,), (1,)), ((), ())), preferred_element_type=jnp.float32)


def kernel(
    docs_hbm, heads_hbm, q_hbm, k_hbm, v_hbm, out_ref, docs, heads, q_ref, k_ref, v_ref, isem,
    kv, over, turn, sink, qx, po, pr, pt, st, sr, res, rin, heads_via, heads_in, hsem, s_ref,
    ksend, krecv, vsend, vrecv, usend, urecv, ssend, srecv, qsend, qrecv, wsend, wrecv, psend, precv, tsend, trecv, osend, orecv,
):
    sec = lax.axis_index("section")
    me = lax.axis_index("seq")
    nsec = lax.axis_size("section")
    fetch = [
        pltpu.make_async_copy(src, dst, isem.at[i])
        for i, (src, dst) in enumerate(
            ((heads_hbm, heads), (k_hbm, k_ref), (v_hbm, v_ref), (docs_hbm, docs), (q_hbm, q_ref))
        )
    ]
    for copy in fetch:
        copy.start()
    nseq = NX * NZ
    x, z = me // NZ, me % NZ
    row_next, row_prev = x * NZ + (z + 1) % NZ, x * NZ + (z + NZ - 1) % NZ
    pos_next, pos_prev = (me + 1) % nseq, (me + nseq - 1) % nseq
    pos_far, pos_back = (me + NZ - 1) % nseq, (me + nseq - NZ + 1) % nseq
    row_up, row_down = (me + NZ) % nseq, (me + nseq - NZ) % nseq
    wrap_next = (me + 1) // nseq
    wrap_prev = 1 - (me + nseq - 1) // nseq
    wrap_far = (me + NZ - 1) // nseq

    barrier = pltpu.get_barrier_semaphore()
    near = [row_next, row_prev, pos_next, pos_prev, pos_far, pos_back]
    near += [(x + e) % NX * NZ + z for e in range(1, NX)]
    for to in near:
        pl.semaphore_signal(barrier, inc=1, device_id={"seq": to}, device_id_type=MESH)
    for by in (1, nsec - 1):
        pl.semaphore_signal(
            barrier, inc=1, device_id={"section": (sec + by) % nsec}, device_id_type=MESH
        )

    for copy in fetch[:3]:
        copy.wait()
    lo = jnp.minimum(heads[0, 0], heads[0, 1])
    hi = jnp.maximum(heads[0, 0], heads[0, 1])

    def peer(c, kind):
        ret = c < RKV
        if kind == "next":
            return jnp.where(ret, row_next, pos_next), jnp.where(ret, 0, wrap_next)
        if kind == "prev":
            return jnp.where(ret, row_prev, pos_prev), jnp.where(ret, 0, wrap_prev)
        return jnp.where(ret, row_prev, pos_far), jnp.where(ret, 0, wrap_far)

    def block_copy(c, half, src, dh, dst, to):
        return pltpu.make_async_remote_copy(
            src_ref=kv.at[c, half, :, src], dst_ref=kv.at[c, dh, :, dst],
            send_sem=ksend.at[c, dst, half], recv_sem=krecv.at[c, dst, dh],
            device_id={"seq": to}, device_id_type=MESH,
        )

    def lies(c, slot, half):
        return jnp.where((c >= RKV) & (me < slot), 1 - half, half)

    def push(c, half, src, dst, kind):
        to, swap = peer(c, kind)
        have = lies(c, src, half)
        block_copy(c, have, src, (have + swap) % 2, dst, to).start()

    def landed(c, half, slot):
        have = lies(c, slot, half)
        block_copy(c, have, slot, have, slot, pos_next).wait_recv()
        give_sink(c, half, slot)

    def over_copy(c, half, slot):
        return pltpu.make_async_remote_copy(
            src_ref=kv.at[c, half, :, slot], dst_ref=over.at[c - RKV, half, slot],
            send_sem=ksend.at[c, slot + 1, half], recv_sem=vrecv.at[c - RKV, half, slot],
            device_id={"seq": (me + NZ) % nseq}, device_id_type=MESH,
        )

    def on_copy(c, half, slot):
        swap = (x == 0).astype(jnp.int32)
        dh = (half + swap) % 2
        return pltpu.make_async_remote_copy(
            src_ref=over.at[c - RKV, half, slot], dst_ref=kv.at[c, dh, :, slot + 1],
            send_sem=vsend.at[c - RKV, half, slot], recv_sem=krecv.at[c, slot + 1, dh],
            device_id={"seq": x * NZ}, device_id_type=MESH,
        )

    def push_next(c, half, slot):
        far_end = (z == NZ - 1) & (c >= RKV)

        @pl.when(far_end)
        def _():
            over_copy(c, half, slot).start()

        @pl.when(jnp.logical_not(far_end))
        def _():
            push(c, half, slot, slot + 1, "next")

    def turn_copy(c, half):
        return pltpu.make_async_remote_copy(
            src_ref=kv.at[c, half, :, 0], dst_ref=turn.at[c - RKV, half],
            send_sem=ksend.at[c, NZ - 1, half], recv_sem=urecv.at[c - RKV, half],
            device_id={"seq": pos_prev}, device_id_type=MESH,
        )

    def turn_up(c, half):
        dh = (half + (x == NX - 1).astype(jnp.int32)) % 2
        return pltpu.make_async_remote_copy(
            src_ref=turn.at[c - RKV, half], dst_ref=kv.at[c, dh, :, NZ - 1],
            send_sem=usend.at[c - RKV, half], recv_sem=krecv.at[c, NZ - 1, dh],
            device_id={"seq": row_up}, device_id_type=MESH,
        )

    def turn_round(c, half):
        return pltpu.make_async_remote_copy(
            src_ref=turn.at[c - RKV, half], dst_ref=kv.at[c, half, :, NZ - 2],
            send_sem=ksend.at[c, NZ - 2, half], recv_sem=krecv.at[c, NZ - 2, half],
            device_id={"seq": row_prev}, device_id_type=MESH,
        )

    def pass_turn(c, half):
        @pl.when((c >= RKV) & (z == 0))
        def _():
            turn_copy(c, half).wait_recv()
            turn_up(c, half).start()
            turn_round(c, half).start()

    def pass_over(c, half, slot):
        @pl.when((c >= RKV) & (z == NZ - 1))
        def _():
            over_copy(c, half, slot).wait_recv()
            on_copy(c, half, slot).start()

    def sink_copy(c, slot, r):
        return pltpu.make_async_remote_copy(
            src_ref=kv.at[c, 0, :, slot], dst_ref=sink.at[c - RKV],
            send_sem=ssend.at[c - RKV, r - 1], recv_sem=srecv.at[c - RKV],
            device_id={"seq": r * NZ + z}, device_id_type=MESH,
        )

    def give_sink(c, half, slot):
        @pl.when((x == 0) & (z == slot) & (c >= RKV) & (half == 0))
        def _():
            for r in range(1, NX):
                sink_copy(c, slot, r).start()

    def q_copy(e, h, src):
        back = e == NX - 1 if src == 0 else h == 1
        return pltpu.make_async_remote_copy(
            src_ref=qx.at[src, h], dst_ref=qx.at[e, h], send_sem=qsend.at[e - 1, h], recv_sem=qrecv.at[e - 1, h],
            device_id={"seq": row_down if back else row_up}, device_id_type=MESH,
        )

    def part_copy(e, h):
        return pltpu.make_async_remote_copy(
            src_ref=po.at[e, h], dst_ref=pr.at[e - 1, h],
            send_sem=psend.at[e - 1, h], recv_sem=precv.at[e - 1, h],
            device_id={"seq": (x + NX - e) % NX * NZ + z}, device_id_type=MESH,
        )

    def part_via(h, to):
        return pltpu.make_async_remote_copy(
            src_ref=po.at[2, h], dst_ref=pt.at[h], send_sem=psend.at[1, h], recv_sem=wrecv.at[h],
            device_id={"seq": to}, device_id_type=MESH,
        )

    def part_on(h, to):
        return pltpu.make_async_remote_copy(
            src_ref=pt.at[h], dst_ref=pr.at[1, h], send_sem=wsend.at[h], recv_sem=precv.at[1, h],
            device_id={"seq": to}, device_id_type=MESH,
        )

    def stat_copy(e, h):
        return pltpu.make_async_remote_copy(
            src_ref=st.at[e, h], dst_ref=sr.at[e - 1, h],
            send_sem=tsend.at[e - 1, h], recv_sem=trecv.at[e - 1, h],
            device_id={"seq": (x + NX - e) % NX * NZ + z}, device_id_type=MESH,
        )

    def out_copy(c):
        return pltpu.make_async_remote_copy(
            src_ref=res.at[c], dst_ref=rin.at[c], send_sem=osend.at[c], recv_sem=orecv.at[c],
            device_id={"section": (sec + 1) % nsec}, device_id_type=MESH,
        )

    def heads_copy():
        return pltpu.make_async_remote_copy(
            src_ref=heads_hbm, dst_ref=heads_via, send_sem=hsem.at[0], recv_sem=hsem.at[1],
            device_id={"section": (sec + 1) % nsec}, device_id_type=MESH,
        )

    def heads_in_copy():
        return pltpu.make_async_copy(heads_via, heads_in, hsem.at[2])

    def head_of(c):
        k = c - RKV
        g = k + (k >= lo).astype(jnp.int32)
        g = g + (g >= hi).astype(jnp.int32)
        return jnp.where(c == 0, heads[0, 0], jnp.where(c == 1, heads[0, 1], g))

    def place_of(g):
        first, second = heads_in[0, 0], heads_in[0, 1]
        low, high = jnp.minimum(first, second), jnp.maximum(first, second)
        run = RKV + g - (g > low).astype(jnp.int32) - (g > high).astype(jnp.int32)
        return jnp.where(g == first, 0, jnp.where(g == second, 1, run))

    def columns(ref, half, g, width):
        rows = pl.ds(pl.multiple_of(half * BLK, BLK), BLK)
        return ref[rows, pl.ds(pl.multiple_of(g * width, HEAD_SIZE), width)]

    def own(ref, half, c, width):
        g = head_of(c)
        if isinstance(c, int) and c < RKV:
            out = columns(ref, half, 0, width)
            for other in range(1, KVH):
                out = lax.select(g == other, columns(ref, half, other, width), out)
            return out
        out = columns(ref, half, c - RKV, width)
        for other in (c - 1, c):
            out = lax.select(g == other, columns(ref, half, other, width), out)
        return out

    def stage(c, _):
        for half in range(2):
            kv[c, half, 0, 0] = own(k_ref, half, c, HEAD_SIZE)
            kv[c, half, 1, 0] = own(v_ref, half, c, HEAD_SIZE)
        return 0

    def stage_q(h):
        for half in range(2):
            rows = own(q_ref, half, h, ROWS)
            for j in range(GQ):
                qx[0, h, half, j * BLK : (j + 1) * BLK] = rows[:, j * HEAD_SIZE : (j + 1) * HEAD_SIZE]

    for c in range(RKV):
        stage(c, 0)
    pl.semaphore_wait(barrier, len(near) + 2)

    def first_sends(c, half):
        push_next(c, half, 0)
        turns = (z == 1) & (c >= RKV)

        @pl.when(turns)
        def _():
            turn_copy(c, half).start()

        @pl.when(jnp.logical_not(turns))
        def _():
            push(c, half, 0, NZ - 1, "far")

        give_sink(c, half, 0)

    for n in range(LEAD):
        first_sends(jnp.int32(n // 2), n % 2)
    for copy in fetch[3:]:
        copy.wait()
    for c in range(RKV):
        stage_q(c)
    for h in range(RKV):
        for e in (1, NX - 1):
            q_copy(e, h, 0).start()
    heads_copy().start()
    lax.fori_loop(RKV, KVH, stage, 0)

    tri = lax.rem(lax.broadcasted_iota(jnp.int32, (ROWS, BLK), 0), BLK) >= lax.broadcasted_iota(
        jnp.int32, (ROWS, BLK), 1
    )

    def bias_of(ok):
        return jnp.where(ok, 0.0, NEG).astype(jnp.float32)

    def attend(queries, tiles):
        top, at, places = None, 0, []
        for keys, _, biases in tiles:
            s = dot_nt(queries, keys())
            for i, b in enumerate(biases):
                piece = s[:, i * BLK : (i + 1) * BLK] + b
                s_ref[:, at + i * BLK : at + (i + 1) * BLK] = piece
                top = piece if top is None else jnp.maximum(top, piece)
            places.append((at, len(biases) * BLK))
            at += len(biases) * BLK
        top = jnp.maximum(jnp.max(top, axis=1, keepdims=True), LOW)
        cut = top * CEXP
        total, mixed = None, None
        for (_, values, _), (at, width) in zip(tiles, places):
            w = jnp.exp2(s_ref[:, at : at + width] * CEXP - cut)
            for i in range(width // BLK):
                piece = w[:, i * BLK : (i + 1) * BLK]
                total = piece if total is None else total + piece
            part = jnp.dot(w.astype(jnp.bfloat16), values(), preferred_element_type=jnp.float32)
            mixed = part if mixed is None else mixed + part
        return top, jnp.sum(total, axis=1, keepdims=True), mixed

    def pair(c, half, which, i):
        return lambda: kv[c, half, which, 2 * i : 2 * i + 2].reshape(2 * BLK, HEAD_SIZE)

    def running(c, half):
        k = c - RKV
        up = half == 1
        rows = own(q_ref, half, c, ROWS)
        queries = jnp.concatenate(
            [rows[:, j * HEAD_SIZE : (j + 1) * HEAD_SIZE] for j in range(GQ)], axis=0
        )
        tiles = [(lambda: sink[k, 0], lambda: sink[k, 1], [bias_of(up | (me >= WBLOCKS))])]
        for i in range(NZ // 2):
            biases = [bias_of(up | (me >= d)) for d in (2 * i, 2 * i + 1)]
            if i == 0:
                biases[0] = jnp.where(tri, 0.0, NEG)
            tiles.append((pair(c, half, 0, i), pair(c, half, 1, i), biases))
        _, total, mixed = attend(queries, tiles)
        out = (mixed / total).astype(jnp.bfloat16)
        for j in range(GQ):
            res[c, pl.ds(pl.multiple_of(half * BLK, BLK), BLK), j * HEAD_SIZE : (j + 1) * HEAD_SIZE] = out[
                j * BLK : (j + 1) * BLK
            ]

    def retrieval(h, e):
        qrow = (x + NX - e) % NX
        for half in range(2):
            i_blk = half * nseq + qrow * NZ + z
            i_doc = docs[0, i_blk]
            tiles = []
            for khalf in range(half + 1):
                for i in range(NZ // 2):
                    biases = []
                    for d in (2 * i, 2 * i + 1):
                        j_blk = khalf * nseq + x * NZ + (z + NZ - d) % NZ
                        b = bias_of((docs[0, j_blk] == i_doc) & (j_blk <= i_blk))
                        if d == 0 and khalf == half:
                            b = jnp.where(tri | (j_blk < i_blk), b, NEG)
                        biases.append(b)
                    tiles.append((pair(h, khalf, 0, i), pair(h, khalf, 1, i), biases))
            top, total, mixed = attend(qx[e, h, half], tiles)
            po[e, h, half] = (mixed / jnp.where(total > 0.0, total, 1.0)).astype(jnp.bfloat16)
            for n, column in enumerate((top, total)):
                wide = jnp.broadcast_to(column, (ROWS, BLK))
                for j in range(GQ):
                    row = (half * GQ + j) * 2 + n
                    st[e, h, row : row + 1, :] = wide[j * BLK : (j + 1) * BLK].T[0:1]

        @pl.when(e > 0)
        def _():
            stat_copy(e, h).start()

        @pl.when((e > 0) & (e != 2))
        def _():
            part_copy(e, h).start()

        @pl.when(e == 2)
        def _():
            part_via(h, jnp.where(h == 0, row_up, row_down)).start()

    def combine(h):
        for e in range(1, NX):
            part_copy(e, h).wait_recv()
            stat_copy(e, h).wait_recv()
        for half in range(2):
            for j in range(GQ):
                row = (half * GQ + j) * 2
                tops = [st[0, h, row : row + 1]] + [sr[e, h, row : row + 1] for e in range(NX - 1)]
                sums = [st[0, h, row + 1 : row + 2]] + [sr[e, h, row + 1 : row + 2] for e in range(NX - 1)]
                best = jnp.maximum(jnp.maximum(tops[0], tops[1]), jnp.maximum(tops[2], tops[3]))
                shares = [jnp.exp2((m - best) * CEXP) * l for m, l in zip(tops, sums)]
                whole = shares[0] + shares[1] + shares[2] + shares[3]
                at = slice(j * BLK, (j + 1) * BLK)
                parts = [po[0, h, half, at]] + [pr[e, h, half, at] for e in range(NX - 1)]
                out = None
                for share, part in zip(shares, parts):
                    weight = jnp.broadcast_to(share / whole, (BLK, BLK)).T
                    term = weight * part.astype(jnp.float32)
                    out = term if out is None else out + term
                res[h, half * BLK : (half + 1) * BLK, at] = out.astype(jnp.bfloat16)
        out_copy(h).start()

    def place(g):
        at = place_of(g)
        out = rin[0]
        for c in sorted({1, max(g, RKV), max(g + 1, RKV), min(g + RKV, KVH - 1)} - {KVH}):
            out = lax.select(at == c, rin[c], out)
        out_ref[:, g * ROWS : (g + 1) * ROWS] = out

    def micro(w, _):
        def with_wave(n, f):
            @pl.when((n >= 0) & (n < WAVES))
            def _():
                f(n // 2, n % 2)

        with_wave(w - DONE, lambda c, half: landed(c, half, 4))

        def third(c, half):
            landed(c, half, 3)

            @pl.when(c < PLUS)
            def _():
                push(c, half, 3, 4, "next")

            landed(c, half, 5)

            @pl.when(c >= PLUS)
            def _():
                push(c, half, 5, 4, "prev")

        with_wave(w - 1 - 2 * LAG, third)

        def second(c, half):
            landed(c, half, 2)
            push(c, half, 2, 3, "next")
            landed(c, half, 6)
            push(c, half, 6, 5, "prev")

        with_wave(w - 1 - LAG, second)

        def first(c, half):
            landed(c, half, 1)
            push_next(c, half, 1)
            landed(c, half, 7)

            @pl.when((z > 0) | (c < RKV))
            def _():
                push(c, half, 7, 6, "prev")


        with_wave(w + LEAD - 2, pass_turn)
        with_wave(w + LEAD - 2, lambda c, half: pass_over(c, half, 0))
        with_wave(w - 2, lambda c, half: pass_over(c, half, 1))
        with_wave(w - 1, first)
        with_wave(w + LEAD, first_sends)

        @pl.when(w == 1)
        def _():
            q_copy(1, 0, 0).wait_recv()
            q_copy(2, 0, 1).start()
            q_copy(NX - 1, 1, 0).wait_recv()
            q_copy(2, 1, NX - 1).start()

        @pl.when((w == DONE + 5) | (w == DONE + 9))
        def _():
            h = (w - DONE - 5) // NX
            part_via(h, row_up).wait_recv()
            part_on(h, jnp.where(h == 0, row_up, row_down)).start()

        @pl.when(w == DONE + 2)
        def _():
            for h in range(RKV):
                q_copy(2, h, 0).wait_recv()
                q_copy(NX - 1 if h == 0 else 1, h, 0).wait_recv()

        @pl.when((w >= DONE + 2) & (w < DONE + 10))
        def _():
            retrieval((w - DONE - 2) // NX, (w - DONE - 1) % NX)

        half = (w + NZ - DONE - 1) % 2
        c = (w + NZ - DONE - 1) // 2 - NZ // 2

        @pl.when((c >= RKV) & (c < KVH))
        def _():
            @pl.when(half == 0)
            def _():
                @pl.when(x == 0)
                def _():
                    sink[c - RKV] = kv[c, 0, :, z]

                @pl.when(x > 0)
                def _():
                    sink_copy(c, 0, 1).wait_recv()

            running(c, half)

            @pl.when(half == 1)
            def _():
                out_copy(c).start()

        @pl.when(w == DONE + 11)
        def _():
            lax.fori_loop(0, RKV, lambda h, _: (combine(h), 0)[1], 0)

        @pl.when(w == DONE + 14)
        def _():
            heads_copy().wait_recv()
            heads_in_copy().start()
            heads_in_copy().wait()
            for c in range(KVH - 2):
                out_copy(c).wait_recv()
            for g in range(KVH - 4):
                place(g)

        return 0

    lax.fori_loop(0, DONE + WAVES + 1, micro, 0)

    for c in range(KVH - 2, KVH):
        out_copy(c).wait_recv()
    for g in range(KVH - 4, KVH):
        place(g)
    for c in range(KVH):
        out_copy(c).wait_send()
    heads_copy().wait_send()

    def finish(c, _):
        for slot in range(1, NZ):
            for half in range(2):
                block_copy(c, half, slot, half, slot, pos_next).wait_send()
        return 0

    lax.fori_loop(0, KVH, finish, 0)
    for e in range(1, NX):
        for h in range(RKV):
            q_copy(e, h, 0).wait_send()
        for h in range(RKV):
            part_copy(e, h).wait_send()
            stat_copy(e, h).wait_send()
    for h in range(RKV):
        part_on(h, row_up).wait_send()

    @pl.when(z == 0)
    def _():
        for c in range(RKV, KVH):
            for half in range(2):
                turn_up(c, half).wait_send()

    @pl.when(z == NZ - 1)
    def _():
        for c in range(RKV, KVH):
            for half in range(2):
                for slot in range(2):
                    on_copy(c, half, slot).wait_send()

    @pl.when(x == 0)
    def _():
        for c in range(RKV, KVH):
            for r in range(1, NX):
                sink_copy(c, 0, r).wait_send()


def shards(query, keys, values, documents, retrieval_heads):
    rows, width = query.shape[1:]
    bf, f32 = jnp.bfloat16, jnp.float32
    dma = pltpu.SemaphoreType.DMA
    vmem = pl.BlockSpec(memory_space=pltpu.VMEM)
    hbm = pl.BlockSpec(memory_space=pltpu.HBM)
    out = pl.pallas_call(
        kernel,
        out_shape=jax.ShapeDtypeStruct((rows, width), bf),
        in_specs=[hbm] * 5,
        out_specs=vmem,
        scratch_shapes=[
            pltpu.SMEM(documents.shape, jnp.int32),
            pltpu.SMEM(retrieval_heads.shape, jnp.int32),
            pltpu.VMEM((rows, width), bf),
            pltpu.VMEM(keys.shape[1:], bf),
            pltpu.VMEM(values.shape[1:], bf),
            dma((5,)),
            pltpu.VMEM((KVH, 2, 2, NZ, BLK, HEAD_SIZE), bf),
            pltpu.VMEM((RUN, 2, 2, 2, BLK, HEAD_SIZE), bf),
            pltpu.VMEM((RUN, 2, 2, BLK, HEAD_SIZE), bf),
            pltpu.VMEM((RUN, 2, BLK, HEAD_SIZE), bf),
            pltpu.VMEM((NX, RKV, 2, ROWS, HEAD_SIZE), bf),
            pltpu.VMEM((NX, RKV, 2, ROWS, HEAD_SIZE), bf),
            pltpu.VMEM((NX - 1, RKV, 2, ROWS, HEAD_SIZE), bf),
            pltpu.VMEM((RKV, 2, ROWS, HEAD_SIZE), bf),
            pltpu.VMEM((NX, RKV, 16, BLK), f32),
            pltpu.VMEM((NX - 1, RKV, 16, BLK), f32),
            pltpu.VMEM((KVH, rows, ROWS), bf),
            pltpu.VMEM((KVH, rows, ROWS), bf),
            pltpu.VMEM(retrieval_heads.shape, jnp.int32),
            pltpu.SMEM(retrieval_heads.shape, jnp.int32),
            dma((3,)),
            pltpu.VMEM((ROWS, 2 * NZ * BLK), f32),
            dma((KVH, NZ, 2)),
            dma((KVH, NZ, 2)),
            dma((RUN, 2, 2)),
            dma((RUN, 2, 2)),
            dma((RUN, 2)),
            dma((RUN, 2)),
            dma((RUN, NX - 1)),
            dma((RUN,)),
            dma((NX - 1, RKV)),
            dma((NX - 1, RKV)),
            dma((RKV,)),
            dma((RKV,)),
            dma((NX - 1, RKV)),
            dma((NX - 1, RKV)),
            dma((NX - 1, RKV)),
            dma((NX - 1, RKV)),
            dma((KVH,)),
            dma((KVH,)),
        ],
        compiler_params=pltpu.CompilerParams(
            collective_id=0, has_side_effects=True, vmem_limit_bytes=56 * 1024 * 1024
        ),
    )(documents, retrieval_heads, query[0], keys[0], values[0])
    return out[None]


def solution(mesh):
    placed = (
        P("section", "seq", None),
        P("section", "seq", None),
        P("section", "seq", None),
        P("section", None),
        P("section", None),
    )
    return jax.shard_map(
        shards, mesh=mesh, in_specs=placed, out_specs=P("section", "seq", None), check_vma=False
    )
```

time: 164 us -> 130 us (0.79)
  the two profiles are of different devices: /device:TPU:10 before, /device:TPU:4 now
where the time goes in v2:
time: 130 us
  Pallas kernels  127 us (98%)
  local copies, waits for them, and re-layouts  2.65 us (2%)
    pallas_call x1, Pallas kernels, shards(): pl.pallas_call(kernel, out_shape=jax.ShapeDtypeStruct((rows, width), bf),...  127 us
    unnamed x1, local copies, waits for them, and re-layouts  2.65 us

profile of v2, /device:TPU:4, one launch (start us, length us, event | category | flops | bytes accessed | tf_op | source)
XLA Modules:
  0.0 130.0 jit_solution(6460019244882717252)
XLA Ops:
  0.0 127.4 %shard_map.55 = bf16[256,3072]{1,0:T(8,128)(2,1)} custom-call(s32[1,64]{1,0:T(1,128)} %docs_hbm.1, s32[1,2]{1,0:T(1,128)} %heads_hbm.1, bf16[256,3072]{1,0:T(8,128)(2,1)} %bitcast.5, bf16[256,1024]{1,0:T(8,128)(2,1)} %bitcast.6, bf16[256,1024]{1,0:T(8,128)(2,1)} %bitcast.7), custom_call_target="tpu_custom_call" | custom-call | tf_op jit(solution)/shard_map/pallas_call | solution.py:573
  127.4 2.7 %copy.7 = bf16[1,256,3072]{2,1,0:T(8,128)(2,1)} copy(bf16[1,256,3072]{2,1,0:T(8,128)(2,1)} %bitcast.4) | data formatting | bytes 3145728

commit v3 on v2

--- a/solution.py
+++ b/solution.py
@@ -18,7 +18,7 @@
 NZ = 8
 NX = 4
 LEAD = 4
-PLUS = 3
+PLUS = 5
 WAVES = 2 * KVH
 LAG = 2
 DONE = 1 + 3 * LAG
@@ -176,12 +176,29 @@
             for r in range(1, NX):
                 sink_copy(c, slot, r).start()
 
-    def q_copy(e, h, src):
-        back = e == NX - 1 if src == 0 else h == 1
-        return pltpu.make_async_remote_copy(
-            src_ref=qx.at[src, h], dst_ref=qx.at[e, h], send_sem=qsend.at[e - 1, h], recv_sem=qrecv.at[e - 1, h],
-            device_id={"seq": row_down if back else row_up}, device_id_type=MESH,
-        )
+    def q_copy(e, h):
+        return pltpu.make_async_remote_copy(
+            src_ref=qx.at[0, h], dst_ref=qx.at[e, h], send_sem=qsend.at[e - 1, h], recv_sem=qrecv.at[e - 1, h],
+            device_id={"seq": row_up if e == 1 else row_down}, device_id_type=MESH,
+        )
+
+    def goes_back(h):
+        return (z == 0) | (h == 1)
+
+    def q_from(h):
+        return jnp.where(goes_back(h), NX - 1, 1)
+
+    def q_on(h):
+        return pltpu.make_async_remote_copy(
+            src_ref=qx.at[q_from(h), h], dst_ref=qx.at[2, h], send_sem=qsend.at[1, h], recv_sem=qrecv.at[1, h],
+            device_id={"seq": jnp.where(goes_back(h), row_down, row_up)}, device_id_type=MESH,
+        )
+
+    def q_wait(e, h):
+        pltpu.make_async_remote_copy(
+            src_ref=qx.at[e, h], dst_ref=qx.at[e, h], send_sem=qsend.at[e - 1, h], recv_sem=qrecv.at[e - 1, h],
+            device_id={"seq": row_up}, device_id_type=MESH,
+        ).wait_recv()
 
     def part_copy(e, h):
         return pltpu.make_async_remote_copy(
@@ -290,7 +307,7 @@
         stage_q(c)
     for h in range(RKV):
         for e in (1, NX - 1):
-            q_copy(e, h, 0).start()
+            q_copy(e, h).start()
     heads_copy().start()
     lax.fori_loop(RKV, KVH, stage, 0)
 
@@ -380,7 +397,7 @@
 
         @pl.when(e == 2)
         def _():
-            part_via(h, jnp.where(h == 0, row_up, row_down)).start()
+            part_via(h, jnp.where(goes_back(h), row_down, row_up)).start()
 
     def combine(h):
         for e in range(1, NX):
@@ -460,22 +477,21 @@
 
         @pl.when(w == 1)
         def _():
-            q_copy(1, 0, 0).wait_recv()
-            q_copy(2, 0, 1).start()
-            q_copy(NX - 1, 1, 0).wait_recv()
-            q_copy(2, 1, NX - 1).start()
+            for h in range(RKV):
+                q_wait(q_from(h), h)
+                q_on(h).start()
 
         @pl.when((w == DONE + 5) | (w == DONE + 9))
         def _():
             h = (w - DONE - 5) // NX
             part_via(h, row_up).wait_recv()
-            part_on(h, jnp.where(h == 0, row_up, row_down)).start()
+            part_on(h, jnp.where(goes_back(h), row_down, row_up)).start()
 
         @pl.when(w == DONE + 2)
         def _():
             for h in range(RKV):
-                q_copy(2, h, 0).wait_recv()
-                q_copy(NX - 1 if h == 0 else 1, h, 0).wait_recv()
+                q_wait(2, h)
+                q_wait(NX - q_from(h), h)
 
         @pl.when((w >= DONE + 2) & (w < DONE + 10))
         def _():
@@ -537,7 +553,7 @@
     lax.fori_loop(0, KVH, finish, 0)
     for e in range(1, NX):
         for h in range(RKV):
-            q_copy(e, h, 0).wait_send()
+            q_copy(e, h).wait_send()
         for h in range(RKV):
             part_copy(e, h).wait_send()
             stat_copy(e, h).wait_send()

time: 130 us -> 122 us (0.938)
  the two profiles are of different devices: /device:TPU:4 before, /device:TPU:1 now
where the time goes in v3:
time: 122 us
  Pallas kernels  120 us (98%)
  local copies, waits for them, and re-layouts  2.65 us (2%)
    pallas_call x1, Pallas kernels, shards(): pl.pallas_call(kernel, out_shape=jax.ShapeDtypeStruct((rows, width), bf),...  120 us
    unnamed x1, local copies, waits for them, and re-layouts  2.65 us

profile of v3, /device:TPU:1, one launch (start us, length us, event | category | flops | bytes accessed | tf_op | source)
XLA Modules:
  0.0 122.3 jit_solution(4866397216131605842)
XLA Ops:
  0.0 119.7 %shard_map.55 = bf16[256,3072]{1,0:T(8,128)(2,1)} custom-call(s32[1,64]{1,0:T(1,128)} %docs_hbm.1, s32[1,2]{1,0:T(1,128)} %heads_hbm.1, bf16[256,3072]{1,0:T(8,128)(2,1)} %bitcast.5, bf16[256,1024]{1,0:T(8,128)(2,1)} %bitcast.6, bf16[256,1024]{1,0:T(8,128)(2,1)} %bitcast.7), custom_call_target="tpu_custom_call" | custom-call | tf_op jit(solution)/shard_map/pallas_call | solution.py:589
  119.7 2.7 %copy.7 = bf16[1,256,3072]{2,1,0:T(8,128)(2,1)} copy(bf16[1,256,3072]{2,1,0:T(8,128)(2,1)} %bitcast.4) | data formatting | bytes 3145728

commit v4 on v3

--- a/solution.py
+++ b/solution.py
@@ -18,7 +18,6 @@
 NZ = 8
 NX = 4
 LEAD = 4
-PLUS = 5
 WAVES = 2 * KVH
 LAG = 2
 DONE = 1 + 3 * LAG
@@ -181,6 +180,9 @@
             src_ref=qx.at[0, h], dst_ref=qx.at[e, h], send_sem=qsend.at[e - 1, h], recv_sem=qrecv.at[e - 1, h],
             device_id={"seq": row_up if e == 1 else row_down}, device_id_type=MESH,
         )
+
+    def goes_on(c):
+        return (c < RKV) | (c % 2 == 0)
 
     def goes_back(h):
         return (z == 0) | (h == 1)
@@ -439,13 +441,13 @@
         def third(c, half):
             landed(c, half, 3)
 
-            @pl.when(c < PLUS)
+            @pl.when(goes_on(c))
             def _():
                 push(c, half, 3, 4, "next")
 
             landed(c, half, 5)
 
-            @pl.when(c >= PLUS)
+            @pl.when(jnp.logical_not(goes_on(c)))
             def _():
                 push(c, half, 5, 4, "prev")
 

time: 122 us -> 124 us (1.016)
    pallas_call x1, Pallas kernels: 120 us -> 121 us  [shards(): pl.pallas_call(kernel, out_shape=jax.ShapeDtypeStruct((rows, width), bf),...]
where the time goes in v4:
time: 124 us
  Pallas kernels  121 us (98%)
  local copies, waits for them, and re-layouts  2.65 us (2%)
    pallas_call x1, Pallas kernels, shards(): pl.pallas_call(kernel, out_shape=jax.ShapeDtypeStruct((rows, width), bf),...  121 us
    unnamed x1, local copies, waits for them, and re-layouts  2.65 us

profile of v4, /device:TPU:1, one launch (start us, length us, event | category | flops | bytes accessed | tf_op | source)
XLA Modules:
  0.0 124.1 jit_solution(11526247854970245325)
XLA Ops:
  0.0 121.5 %shard_map.55 = bf16[256,3072]{1,0:T(8,128)(2,1)} custom-call(s32[1,64]{1,0:T(1,128)} %docs_hbm.1, s32[1,2]{1,0:T(1,128)} %heads_hbm.1, bf16[256,3072]{1,0:T(8,128)(2,1)} %bitcast.5, bf16[256,1024]{1,0:T(8,128)(2,1)} %bitcast.6, bf16[256,1024]{1,0:T(8,128)(2,1)} %bitcast.7), custom_call_target="tpu_custom_call" | custom-call | tf_op jit(solution)/shard_map/pallas_call | solution.py:591
  121.5 2.7 %copy.7 = bf16[1,256,3072]{2,1,0:T(8,128)(2,1)} copy(bf16[1,256,3072]{2,1,0:T(8,128)(2,1)} %bitcast.4) | data formatting | bytes 3145728
